TPU v7x, 128 devices: a whole 4x4x4 slice. The times are simulated.
128 devices in a mesh: dp: 8 (over x_hi, z), tensor: 16 (over x_lo, y, core).
Axes of the slice: x: 4 (x_hi: 2, x_lo: 2; x = x_hi * 2 + x_lo), y: 4, z: 4, core: 2. Of those that a mesh axis runs over, the one named last changes fastest.
Arguments:
- ckpt_values: bfloat16 [2048, 18432], P(('dp', 'tensor')), may hold values from -6 to 6
- ckpt_scales: bfloat16 [2048, 144], P(('dp', 'tensor')), may hold values from 0.25 to 4
- norm_gain: float32 [18432], replicated, may hold values from 0.5 to 1.5
- pre_act: bfloat16 [2048, 36864], P('dp', 'tensor'), may hold values from -6 to 6
- act_grad: bfloat16 [2048, 36864], P('dp', 'tensor'), may hold values from -0.09375 to 0.09375
Outputs:
- weight_grad: bfloat16 [18432, 36864], P('dp', 'tensor')
All inputs are finite; a program needn't handle non-finite values.
Results may differ from a plain program's by a relative error of at most 0.0057.
Values may be sent and summed in bfloat16 or wider, within the bound.
A program may use at most 128 MiB of HBM per device.

v0:
```python
import jax
import jax.numpy as jnp
from jax import lax
from jax.sharding import PartitionSpec as P

QB = 128


def normalize(values, scales, gain):
    count = values.shape[0]
    width = values.shape[1]
    inputs = (
        values.astype(jnp.float32).reshape(count, width // QB, QB)
        * scales.astype(jnp.float32)[:, :, None]
    )
    inputs = inputs.reshape(count, width)
    inverse = lax.rsqrt(jnp.mean(inputs * inputs, axis=1, keepdims=True) + 1e-05)
    return (inputs * inverse * gain).astype(jnp.bfloat16)


def on_device(ckpt_values, ckpt_scales, norm_gain, pre_act, act_grad):
    pre_grad = (
        act_grad.astype(jnp.float32) * 2.0 * jnp.maximum(pre_act.astype(jnp.float32), 0.0)
    ).astype(jnp.bfloat16)
    normed = normalize(ckpt_values, ckpt_scales, norm_gain)
    gathered = lax.all_gather(normed, "tensor", axis=0, tiled=True)
    grouped = lax.all_to_all(gathered[None], "dp", split_axis=2, concat_axis=0, tiled=True)
    features = grouped.reshape(grouped.shape[0] * grouped.shape[1], grouped.shape[2])
    total = lax.dot_general(
        features,
        lax.all_gather(pre_grad, "dp", axis=0, tiled=True),
        (((0,), (0,)), ((), ())),
        preferred_element_type=jnp.float32,
    )
    return total.astype(jnp.bfloat16)


def solution(mesh):
    in_specs = (
        P(("dp", "tensor"), None),
        P(("dp", "tensor"), None),
        P(),
        P("dp", "tensor"),
        P("dp", "tensor"),
    )
    out_specs = P("dp", "tensor")
    return jax.shard_map(
        on_device, mesh=mesh, in_specs=in_specs, out_specs=out_specs, check_vma=False
    )
```

profile of v0, /device:TPU:0, one launch (start us, length us, event | category | flops | bytes accessed | tf_op | source)
XLA Modules:
  0.0 405.1 jit_solution(7969495020714175538)
XLA Ops:
  6.5 0.0 copy-start
  6.5 0.0 copy-start.3
  6.5 0.0 all-gather.3.cloned.1.call-start
  6.5 1.1 mul.39
  7.7 0.0 copy-start.1
  7.7 0.0 copy-start.2
  7.7 1.7 multiply_reduce_fusion
  9.4 0.0 copy-done
  9.4 0.0 copy-done.3
  9.4 1.3 multiply_convert_fusion.1
  10.7 0.0 all-gather.3.cloned.1.call-update
  10.7 0.0 all-gather.5.cloned.1.call-start
  10.7 0.0 copy-done.1
  10.8 0.0 copy-done.2
  10.8 1.5 multiply_convert_fusion
  12.2 0.0 all-gather.5.cloned.1.call-update
  12.2 58.1 %all-gather.3.cloned.1.call-done = bf16[256,18432]{1,0:T(8,128)(2,1)} async-done(((bf16[16,18432]{1,0:T(8,128)(2,1)}), bf16[256,18432]{1,0:T(8,128)(2,1)}) %all-gather.3.cloned.1.call-update) | async-done | bytes 9437200 | tf_op jit(solution)/shard_map/all_gather | solution.py:26
  70.3 38.5 %copy.9 = bf16[1,256,18432]{1,0,2:T(2,128)(2,1)} copy(bf16[1,256,18432]{2,1,0:T(8,128)(2,1)} %bitcast.21) | data formatting | bytes 18874368 | tf_op jit(solution)/shard_map/broadcast_in_dim | solution.py:27
  108.8 0.5 broadcast.24
  109.4 95.0 %reduce = bf16[18432,256]{1,0:T(8,128)(2,1)} reduce(bf16[18432,1,256]{2,1,0:T(2,128)(2,1)} %bitcast.17, bf16[]{:T(256)} %broadcast.24), dimensions={1}, to_apply=%bitcast.12.reduce_sub_computation | reduce | bytes 18874370
  204.4 10.4 %reshape.18 = bf16[8,2,294912]{2,1,0:T(2,128)(2,1)} reshape(bf16[18432,256]{1,0:T(8,128)(2,1)} %reduce) | data formatting | bytes 18874368
  214.8 114.4 %all_to_all.15 = bf16[8,2,294912]{2,1,0:T(2,128)(2,1)} all-to-all(bf16[8,2,294912]{2,1,0:T(2,128)(2,1)} %reshape.18), channel_id=1, replica_groups=mesh['dp'=8,'tensor'=16] {'dp'}, dimensions={0} | all-to-all | bytes 18874368 | tf_op jit(solution)/shard_map/all_to_all | solution.py:27
  329.2 14.5 %reshape.19 = bf16[18432,1,256]{2,1,0:T(2,128)(2,1)} reshape(bf16[8,2,294912]{2,1,0:T(2,128)(2,1)} %all_to_all.15) | data formatting | bytes 18874368
  343.7 12.7 %copy.11 = bf16[1,256,18432]{1,2,0:T(8,128)(2,1)} copy(bf16[1,256,18432]{1,0,2:T(2,128)(2,1)} %bitcast.16) | data formatting | bytes 18874368
  356.4 12.6 %copy.10 = bf16[8,1,256,2304]{3,2,0,1:T(8,128)(2,1)} copy(bf16[8,1,256,2304]{2,3,0,1:T(8,128)(2,1)} %bitcast.18) | data formatting | bytes 18874368 | tf_op jit(solution)/shard_map/all_to_all | solution.py:27
  369.0 0.0 all-gather.5.cloned.1.call-done
  369.0 29.3 %convolution_convert_fusion = bf16[2304,2304]{1,0:T(8,128)(2,1)} fusion(bf16[2048,2304]{1,0:T(8,128)(2,1)} %bitcast.22, bf16[2048,2304]{1,0:T(8,128)(2,1)} %all-gather.5.cloned.1.call-done), kind=kOutput, calls=%fused_computation | convolution fusion | flops 21748580352 | bytes 29491200 | tf_op jit(solution)/shard_map/dot_general | solution.py:29
  (1 shorter events, 0.0 us)
Async XLA Ops:
  6.5 2.9 copy-start
  6.5 2.9 copy-start.3
  6.5 63.8 %all-gather.3.cloned.1.call-start = ((), (), s32[]{:S(2)}) async-start(), calls=%async_computation.1 | async-start | bytes 10027008 | tf_op jit(solution)/shard_map/all_gather | solution.py:26
  7.7 3.1 copy-start.1
  7.7 3.1 copy-start.2
  10.7 358.3 %all-gather.5.cloned.1.call-start = ((), (), s32[]{:S(2)}) async-start(), calls=%async_computation.2 | async-start | bytes 10616832 | tf_op jit(solution)/shard_map/all_gather | solution.py:31
Sparse Core Ops, SparseCore 0:
  10.8 59.4 all-gather.2
  72.6 117.6 all-gather.4
where the time goes:
time: 407 us; the launch traced here: 405 us
  blocking collectives  114 us (28%)
  other arithmetic  99.5 us (24%)
  local copies, waits for them, and re-layouts  90.3 us (22%)
  waiting for transfers between devices  58.1 us (14%)
  matrix products  29.3 us (7%)
  between operations  13.5 us (3%)
    all_to_all x1, blocking collectives, on_device(): lax.all_to_all(gathered[None], 'dp', split_axis=2, concat_axis=0, tiled=T...  114 us
    unnamed x1, other arithmetic  95 us
    all_gather x1, waiting for transfers between devices, on_device(): gathered = lax.all_gather(normed, 'tensor', axis=0, tiled=True)  58.1 us
    broadcast_in_dim x1, local copies, waits for them, and re-layouts, on_device(): gathered[None]  38.5 us
    unnamed x12, local copies, waits for them, and re-layouts  38.1 us
    dot_general x1, matrix products, on_device(): lax.dot_general(features, lax.all_gather(pre_grad, 'dp', axis=0, tiled=Tr...  29.3 us
    all_to_all x1, local copies, waits for them, and re-layouts, on_device(): lax.all_to_all(gathered[None], 'dp', split_axis=2, concat_axis=0, tiled=T...  12.6 us
  transfers between devices with their start and end apart: 2, of which 1 were waited for; matrix products, arithmetic and copies ran while one was open for 46% of the time, Pallas kernels for 0%

commit v1 on v0

--- a/solution.py
+++ b/solution.py
@@ -23,7 +23,9 @@
         act_grad.astype(jnp.float32) * 2.0 * jnp.maximum(pre_act.astype(jnp.float32), 0.0)
     ).astype(jnp.bfloat16)
     normed = normalize(ckpt_values, ckpt_scales, norm_gain)
-    gathered = lax.all_gather(normed, "tensor", axis=0, tiled=True)
+    gathered = jnp.concatenate(
+        lax.all_to_all(jnp.stack([normed] * lax.axis_size("tensor")), "tensor", 0, 0), axis=0
+    )
     grouped = lax.all_to_all(gathered[None], "dp", split_axis=2, concat_axis=0, tiled=True)
     features = grouped.reshape(grouped.shape[0] * grouped.shape[1], grouped.shape[2])
     total = lax.dot_general(

time: 407 us -> 545 us (1.34); the launches traced: 405 us -> 535 us
  waiting for transfers between devices: 58.1 us -> 177 us
  starting transfers between devices: 0.04 us -> 5.8 us
    all_to_all x0 -> x1, waiting for transfers between devices: none -> 177 us  [on_device(): lax.all_to_all(jnp.stack([normed] * lax.axis_size('tensor')), 'tensor', 0...]
    all_gather x1 -> x0, waiting for transfers between devices: 58.1 us -> none  [on_device(): gathered = lax.all_gather(normed, 'tensor', axis=0, tiled=True)]
    another operation x0 -> x2, local copies, waits for them, and re-layouts: none -> 43.1 us  [the longest x1 38.3 us: on_device(): gathered[None]]
    broadcast_in_dim x1 -> x0, local copies, waits for them, and re-layouts: 38.5 us -> none  [on_device(): gathered[None]]
    all_to_all x0 -> x1, starting transfers between devices: none -> 5.76 us  [on_device(): lax.all_to_all(jnp.stack([normed] * lax.axis_size('tensor')), 'tensor', 0...]
  transfers between devices with their start and end apart: 2 -> 2, of which waited for: 1 -> 1; matrix products, arithmetic and copies ran while one was open for 46% -> 35% of each run, Pallas kernels for 0% -> 0%
where the time goes in v1:
time: 545 us; the launch traced here: 535 us
  waiting for transfers between devices  177 us (32%)
  blocking collectives  115 us (21%)
  other arithmetic  98.4 us (18%)
  local copies, waits for them, and re-layouts  95.2 us (17%)
  matrix products  29.3 us (5%)
  between operations  13.5 us (2%)
  starting transfers between devices  5.8 us (1%)
    all_to_all x1, waiting for transfers between devices, on_device(): lax.all_to_all(jnp.stack([normed] * lax.axis_size('tensor')), 'tensor', 0...  177 us
    all_to_all x1, blocking collectives, on_device(): lax.all_to_all(gathered[None], 'dp', split_axis=2, concat_axis=0, tiled=T...  115 us
    unnamed x1, other arithmetic  95 us
    another operation x1, local copies, waits for them, and re-layouts, on_device(): gathered[None]  38.3 us
    unnamed x12, local copies, waits for them, and re-layouts  38.1 us
    dot_general x1, matrix products, on_device(): lax.dot_general(features, lax.all_gather(pre_grad, 'dp', axis=0, tiled=Tr...  29.3 us
    all_to_all x1, local copies, waits for them, and re-layouts, on_device(): lax.all_to_all(gathered[None], 'dp', split_axis=2, concat_axis=0, tiled=T...  12.9 us
  transfers between devices with their start and end apart: 2, of which 1 were waited for; matrix products, arithmetic and copies ran while one was open for 35% of the time, Pallas kernels for 0%

profile of v1, /device:TPU:0, one launch (start us, length us, event | category | flops | bytes accessed | tf_op | source)
XLA Modules:
  0.0 534.6 jit_solution(686122364017184653)
XLA Ops:
  6.5 0.0 copy-start
  6.5 0.0 copy-start.3
  6.5 1.1 mul.39
  7.7 1.6 multiply_reduce_fusion
  9.2 0.0 copy-done
  9.2 0.0 copy-done.3
  9.2 0.4 multiply_convert_fusion.1
  9.7 4.8 stack.2
  14.5 0.0 copy-start.1
  14.5 0.0 copy-start.2
  14.5 5.8 %all-to-all-start = ((bf16[16,16,18432]{2,1,0:T(8,128)(2,1)}), bf16[16,16,18432]{2,1,0:T(8,128)(2,1)}, u32[]{:S(2)}, u32[]{:S(2)}) async-start(bf16[16,16,18432]{2,1,0:T(8,128)(2,1)} %stack.2), calls=%async_computation | async-start | bytes 18874368 | tf_op jit(solution)/shard_map/all_to_all | solution.py:27
  20.2 0.0 all-gather.2.cloned.1.call-start
  20.3 0.0 copy-done.1
  20.3 0.0 copy-done.2
  20.3 1.4 multiply_convert_fusion
  21.7 0.0 all-gather.2.cloned.1.call-update
  21.8 177.4 %all-to-all-done = bf16[16,16,18432]{2,1,0:T(8,128)(2,1)} async-done(((bf16[16,16,18432]{2,1,0:T(8,128)(2,1)}), bf16[16,16,18432]{2,1,0:T(8,128)(2,1)}, u32[]{:S(2)}, u32[]{:S(2)}) %all-to-all-start) | async-done | bytes 9437216 | tf_op jit(solution)/shard_map/all_to_all | solution.py:27
  199.2 38.3 %copy.10 = bf16[1,256,18432]{1,0,2:T(2,128)(2,1)} copy(bf16[1,256,18432]{2,1,0:T(8,128)(2,1)} %bitcast) | data formatting | bytes 18874368 | tf_op jit(solution)/shard_map/broadcast_in_dim;reshape | solution.py:29
  237.5 0.5 broadcast.26
  237.9 95.0 %reduce = bf16[18432,256]{1,0:T(8,128)(2,1)} reduce(bf16[18432,1,256]{2,1,0:T(2,128)(2,1)} %bitcast.17, bf16[]{:T(256)} %broadcast.26), dimensions={1}, to_apply=%bitcast.12.reduce_sub_computation | reduce | bytes 18874370
  332.9 10.4 %reshape.20 = bf16[8,2,294912]{2,1,0:T(2,128)(2,1)} reshape(bf16[18432,256]{1,0:T(8,128)(2,1)} %reduce) | data formatting | bytes 18874368
  343.3 115.1 %all_to_all.20 = bf16[8,2,294912]{2,1,0:T(2,128)(2,1)} all-to-all(bf16[8,2,294912]{2,1,0:T(2,128)(2,1)} %reshape.20), channel_id=1, replica_groups=mesh['dp'=8,'tensor'=16] {'dp'}, dimensions={0} | all-to-all | bytes 18874368 | tf_op jit(solution)/shard_map/all_to_all | solution.py:29
  458.4 14.5 %reshape.21 = bf16[18432,1,256]{2,1,0:T(2,128)(2,1)} reshape(bf16[8,2,294912]{2,1,0:T(2,128)(2,1)} %all_to_all.20) | data formatting | bytes 18874368
  472.9 12.7 %copy.12 = bf16[1,256,18432]{1,2,0:T(8,128)(2,1)} copy(bf16[1,256,18432]{1,0,2:T(2,128)(2,1)} %bitcast.16) | data formatting | bytes 18874368
  485.7 12.9 %copy.11 = bf16[8,1,256,2304]{3,2,0,1:T(8,128)(2,1)} copy(bf16[8,1,256,2304]{2,3,0,1:T(8,128)(2,1)} %bitcast.18) | data formatting | bytes 18874368 | tf_op jit(solution)/shard_map/all_to_all | solution.py:29
  498.5 0.0 all-gather.2.cloned.1.call-done
  498.5 29.3 %convolution_convert_fusion = bf16[2304,2304]{1,0:T(8,128)(2,1)} fusion(bf16[2048,2304]{1,0:T(8,128)(2,1)} %bitcast.21, bf16[2048,2304]{1,0:T(8,128)(2,1)} %all-gather.2.cloned.1.call-done), kind=kOutput, calls=%fused_computation | convolution fusion | flops 21748580352 | bytes 29491200 | tf_op jit(solution)/shard_map/dot_general | solution.py:31
  (1 shorter events, 0.0 us)
Async XLA Ops:
  6.5 2.7 copy-start
  6.5 2.7 copy-start.3
  14.5 5.8 %copy-start.1 = (bf16[256,2304]{1,0:T(8,128)(2,1)S(1)}, bf16[256,2304]{1,0:T(8,128)(2,1)}, u32[]{:S(2)}) copy-start(bf16[256,2304]{1,0:T(8,128)(2,1)} %param.8) | copy-start | bytes 3538948
  14.5 5.8 %copy-start.2 = (bf16[256,2304]{1,0:T(8,128)(2,1)S(1)}, bf16[256,2304]{1,0:T(8,128)(2,1)}, u32[]{:S(2)}) copy-start(bf16[256,2304]{1,0:T(8,128)(2,1)} %param.9) | copy-start | bytes 3538948
  14.5 184.7 %all-to-all-start = ((bf16[16,16,18432]{2,1,0:T(8,128)(2,1)}), bf16[16,16,18432]{2,1,0:T(8,128)(2,1)}, u32[]{:S(2)}, u32[]{:S(2)}) async-start(bf16[16,16,18432]{2,1,0:T(8,128)(2,1)} %stack.2), calls=%async_computation | async-start | bytes 18874368 | tf_op jit(solution)/shard_map/all_to_all | solution.py:27
  20.2 478.3 %all-gather.2.cloned.1.call-start = ((), (), s32[]{:S(2)}) async-start(), calls=%async_computation.2 | async-start | bytes 10616832 | tf_op jit(solution)/shard_map/all_gather | solution.py:33
Sparse Core Ops, SparseCore 0:
  23.4 182.9 all-gather.1

commit v2 on v0

--- a/solution.py
+++ b/solution.py
@@ -24,7 +24,12 @@
     ).astype(jnp.bfloat16)
     normed = normalize(ckpt_values, ckpt_scales, norm_gain)
     gathered = lax.all_gather(normed, "tensor", axis=0, tiled=True)
-    grouped = lax.all_to_all(gathered[None], "dp", split_axis=2, concat_axis=0, tiled=True)
+    grouped = jnp.concatenate(
+        lax.all_to_all(
+            jnp.stack(jnp.split(gathered[None], lax.axis_size("dp"), axis=2)), "dp", 0, 0
+        ),
+        axis=0,
+    )
     features = grouped.reshape(grouped.shape[0] * grouped.shape[1], grouped.shape[2])
     total = lax.dot_general(
         features,

time: 407 us -> 328 us (0.81)
  waiting for transfers between devices: 58.1 us -> 254 us
  blocking collectives: 114 us -> 0 us
  other arithmetic: 99.5 us -> 6.96 us
  local copies, waits for them, and re-layouts: 90.3 us -> 15.8 us
  starting transfers between devices: 0.04 us -> 6.88 us
    all_gather x1, waiting for transfers between devices: 0.01 us -> 198 us  [on_device(): lax.all_gather(pre_grad, 'dp', axis=0, tiled=True)]
    all_to_all x1 -> x0, blocking collectives: 114 us -> none  [on_device(): lax.all_to_all(gathered[None], 'dp', split_axis=2, concat_axis=0, tiled=T...]
    unnamed x1 -> x0, other arithmetic: 95 us -> none
    broadcast_in_dim x1 -> x0, local copies, waits for them, and re-layouts: 38.5 us -> none  [on_device(): gathered[None]]
    unnamed x12 -> x9, local copies, waits for them, and re-layouts: 38.1 us -> 13.7 us
    all_to_all x1 -> x0, local copies, waits for them, and re-layouts: 12.6 us -> none  [on_device(): lax.all_to_all(gathered[None], 'dp', split_axis=2, concat_axis=0, tiled=T...]
    all_to_all x0 -> x1, starting transfers between devices: none -> 6.84 us  [on_device(): lax.all_to_all(jnp.stack(jnp.split(gathered[None], lax.axis_size('dp'), a...]
  transfers between devices with their start and end apart: 2 -> 3, of which waited for: 1 -> 2; matrix products, arithmetic and copies ran while one was open for 46% -> 5% of each run, Pallas kernels for 0% -> 0%
where the time goes in v2:
time: 328 us; the launch traced here: 327 us
  waiting for transfers between devices  254 us (77%)
  matrix products  29.3 us (9%)
  local copies, waits for them, and re-layouts  15.8 us (5%)
  between operations  13.4 us (4%)
  other arithmetic  6.96 us (2%)
  starting transfers between devices  6.88 us (2%)
    all_gather x1, waiting for transfers between devices, on_device(): lax.all_gather(pre_grad, 'dp', axis=0, tiled=True)  198 us
    all_gather x1, waiting for transfers between devices, on_device(): gathered = lax.all_gather(normed, 'tensor', axis=0, tiled=True)  56.5 us
    dot_general x1, matrix products, on_device(): lax.dot_general(features, lax.all_gather(pre_grad, 'dp', axis=0, tiled=Tr...  29.3 us
    unnamed x9, local copies, waits for them, and re-layouts  13.7 us
    all_to_all x1, starting transfers between devices, on_device(): lax.all_to_all(jnp.stack(jnp.split(gathered[None], lax.axis_size('dp'), a...  6.84 us
  transfers between devices with their start and end apart: 3, of which 2 were waited for; matrix products, arithmetic and copies ran while one was open for 5% of the time, Pallas kernels for 0%

profile of v2, /device:TPU:0, one launch (start us, length us, event | category | flops | bytes accessed | tf_op | source)
XLA Modules:
  0.0 326.8 jit_solution(11213551635989437401)
XLA Ops:
  6.5 0.0 all-gather.3.cloned.1.call-start
  6.5 1.1 mul.39
  7.6 1.6 multiply_reduce_fusion
  9.2 2.3 multiply_convert_fusion.1
  11.5 0.0 all-gather.3.cloned.1.call-update
  11.5 0.0 all-gather.5.cloned.1.call-start
  11.6 3.1 multiply_convert_fusion
  14.6 0.0 all-gather.5.cloned.1.call-update
  14.7 56.5 %all-gather.3.cloned.1.call-done = bf16[256,18432]{1,0:T(8,128)(2,1)} async-done(((bf16[16,18432]{1,0:T(8,128)(2,1)}), bf16[256,18432]{1,0:T(8,128)(2,1)}) %all-gather.3.cloned.1.call-update) | async-done | bytes 9437200 | tf_op jit(solution)/shard_map/all_gather | solution.py:26
  71.2 0.0 copy-start
  71.2 2.5 fusion.7
  73.7 3.1 fusion.6
  76.8 2.4 fusion.5
  79.1 2.4 fusion.4
  81.5 0.0 copy-done
  81.5 1.1 fusion.3
  82.6 1.1 fusion.2
  83.7 1.1 fusion.1
  84.8 1.1 fusion
  85.9 6.8 %all-to-all-start = ((bf16[8,1,256,2304]{3,2,1,0:T(8,128)(2,1)}), bf16[8,1,256,2304]{3,2,1,0:T(8,128)(2,1)}, u32[]{:S(2)}, u32[]{:S(2)}) async-start(bf16[8,1,256,2304]{3,2,1,0:T(8,128)(2,1)} %fusion), calls=%async_computation | async-start | bytes 18874368 | tf_op jit(solution)/shard_map/all_to_all | solution.py:28
  92.8 197.9 %all-gather.5.cloned.1.call-done = bf16[2048,2304]{1,0:T(8,128)(2,1)} async-done(((bf16[256,2304]{1,0:T(8,128)(2,1)}), bf16[2048,2304]{1,0:T(8,128)(2,1)}) %all-gather.5.cloned.1.call-update) | async-done | bytes 9437200 | tf_op jit(solution)/shard_map/all_gather | solution.py:36
  290.7 0.0 all-to-all-done
  290.7 29.3 %convolution_convert_fusion = bf16[2304,2304]{1,0:T(8,128)(2,1)} fusion(bf16[2048,2304]{1,0:T(8,128)(2,1)} %bitcast.9, bf16[2048,2304]{1,0:T(8,128)(2,1)} %all-gather.5.cloned.1.call-done), kind=kOutput, calls=%fused_computation | convolution fusion | flops 21748580352 | bytes 29491200 | tf_op jit(solution)/shard_map/dot_general | solution.py:34
  (1 shorter events, 0.0 us)
Async XLA Ops:
  6.5 64.6 %all-gather.3.cloned.1.call-start = ((), (), s32[]{:S(2)}) async-start(), calls=%async_computation.1 | async-start | bytes 10027008 | tf_op jit(solution)/shard_map/all_gather | solution.py:26
  11.5 279.2 %all-gather.5.cloned.1.call-start = ((), (), s32[]{:S(2)}) async-start(), calls=%async_computation.2 | async-start | bytes 10616832 | tf_op jit(solution)/shard_map/all_gather | solution.py:36
  71.2 10.3 %copy-start = (bf16[256,18432]{1,0:T(8,128)(2,1)S(1)}, bf16[256,18432]{1,0:T(8,128)(2,1)}, u32[]{:S(2)}) copy-start(bf16[256,18432]{1,0:T(8,128)(2,1)} %all-gather.3.cloned.1.call-done) | copy-start | bytes 28311556
  85.9 204.8 %all-to-all-start = ((bf16[8,1,256,2304]{3,2,1,0:T(8,128)(2,1)}), bf16[8,1,256,2304]{3,2,1,0:T(8,128)(2,1)}, u32[]{:S(2)}, u32[]{:S(2)}) async-start(bf16[8,1,256,2304]{3,2,1,0:T(8,128)(2,1)} %fusion), calls=%async_computation | async-start | bytes 18874368 | tf_op jit(solution)/shard_map/all_to_all | solution.py:28
Sparse Core Ops, SparseCore 0:
  11.6 59.4 all-gather.2
  73.5 217.1 all-gather.4
